TPU v7x, 32 devices: a whole 2x2x4 slice. The times are simulated.
32 devices in a mesh: groups: 2 (over y), rows: 4 (over z), dates: 2 (over x), cols: 2 (over core).
Axes of the slice: x: 2, y: 2, z: 4, core: 2. Of those that a mesh axis runs over, the one named last changes fastest.
Arguments:
- images: bfloat16 [4, 13, 64, 1024], P('dates', None, ('groups', 'rows'), 'cols'), parts along dimension 2, may hold values from -6 to 6
- cloud_mask: int32 [4, 64, 1024], P(None, ('groups', 'rows', 'dates'), 'cols'), parts along dimension 1, may hold values 0 or 1
- counts: int32 [64, 1024], P(('groups', 'rows', 'dates'), 'cols'), parts along dimension 0, may hold values from 1 to 4
- day_of_year: int32 [8], P('groups'), parts along dimension 0, may hold values from 0 to 365
- w_first: bfloat16 [3, 3, 13, 128], replicated, may hold values from -0.5 to 0.5
- b_first: float32 [128], replicated, may hold values from -1.75 to 1.75
- w_second: bfloat16 [3, 3, 128, 128], replicated, may hold values from -0.25 to 0.25
- b_second: float32 [128], replicated, may hold values from -1.75 to 1.75
- w_third: bfloat16 [3, 3, 128, 128], replicated, may hold values from -0.25 to 0.25
- b_third: float32 [128], replicated, may hold values from -1.75 to 1.75
- w_in: bfloat16 [128, 256], replicated, may hold values from -0.75 to 0.75
- w_key: bfloat16 [256, 64], replicated, may hold values from -0.375 to 0.375
- master_query: float32 [16, 4], replicated, may hold values from -8 to 8
- w_mlp: bfloat16 [256, 128], replicated, may hold values from -0.5 to 0.5
- b_mlp: float32 [128], replicated, may hold values from -1.75 to 1.75
- w_dec: bfloat16 [3, 3, 128, 128], replicated, may hold values from -0.25 to 0.25
- b_dec: float32 [128], replicated, may hold values from -1.75 to 1.75
- w_out: bfloat16 [13, 128], replicated, may hold values from -0.75 to 0.75
- b_out: float32 [13], replicated, may hold values from -3 to 3
Outputs:
- prediction: float32 [13, 64, 1024], P(None, ('groups', 'rows', 'dates'), 'cols'), parts along dimension 1
There are 2 independent parts, one for each index of `groups`. A program takes and returns all parts, laid end to end along the dimension named above; an argument that names none is the same for every part. Nothing has to cross between parts.
All inputs are finite; a program needn't handle non-finite values. No bound on the sum of `cloud_mask` on one device may be relied on, other than what follows from the above.
Results may differ from a plain program's by a relative error of at most 0.012.
Values may be sent and summed in bfloat16 or wider, within the bound.
A program may use at most 64 MiB of HBM per device.

v0:
```python
import functools
import math

import jax
import jax.numpy as jnp
import numpy as np
from jax import lax
from jax.experimental import pallas as pl
from jax.experimental.pallas import tpu as pltpu
from jax.sharding import PartitionSpec as P

SIDE = 16
BF = jnp.bfloat16
F32 = jnp.float32


def positions(day_of_year, width_model):
    channel = jnp.arange(width_model // 2).astype(F32)
    frequency = jnp.power(F32(1000.0), -2.0 * channel / width_model)
    angle_table = day_of_year.astype(F32)[:, None] * frequency[None, :]
    return jnp.stack([jnp.sin(angle_table), jnp.cos(angle_table)], axis=-1).reshape(
        day_of_year.shape[0], width_model
    )


def dot(a, b):
    return jnp.dot(a, b, preferred_element_type=F32)


def dot_tn(a, b):
    return lax.dot_general(a, b, (((0,), (0,)), ((), ())), preferred_element_type=F32)


def dot_nt(a, b):
    return lax.dot_general(a, b, (((1,), (1,)), ((), ())), preferred_element_type=F32)


def kernel(
    cfg,
    img_ref,
    mk_ref,
    perm_ref,
    pos_ref,
    w1_ref,
    b1_ref,
    w2_ref,
    b2_ref,
    w3_ref,
    b3_ref,
    win_ref,
    wkey_ref,
    q_ref,
    ex_ref,
    bsel_ref,
    wmlp_ref,
    bmlp_ref,
    wdec_ref,
    bdec_ref,
    wout_ref,
    bout_ref,
    out_ref,
    mine,
    xbuf,
    mkb,
    xw,
    s1,
    s2,
    s3,
    enc,
    pa,
    k1,
    k2,
    k3,
    kd,
    ws,
    sel,
    send_sem,
    recv_sem,
    mask_send,
    mask_recv,
):
    (R, D, dl, own, strip, wdev, heads, model, bands) = cfg
    T = D * dl
    L = T * heads
    M = wdev + 2 * SIDE
    half = strip // 2
    r = lax.axis_index("rows")
    d = lax.axis_index("dates")
    c = lax.axis_index("cols")
    cp = 1 - c
    f = r * D + d
    height = R * strip

    mine[...] = jnp.zeros_like(mine)
    xbuf[...] = jnp.zeros_like(xbuf)
    mkb[...] = jnp.zeros_like(mkb)

    barrier = pltpu.get_barrier_semaphore()

    def greet(rr, others_only):
        for k in range(D):
            for other in range(2):
                if others_only and k == 0 and other == 0:
                    continue
                pl.semaphore_signal(
                    barrier,
                    inc=1,
                    device_id={
                        "rows": rr,
                        "dates": lax.rem(d + k, D),
                        "cols": cp if other else c,
                    },
                    device_id_type=pl.DeviceIdType.MESH,
                )

    greet(r, True)

    @pl.when(r > 0)
    def _():
        greet(r - 1, False)

    @pl.when(r < R - 1)
    def _():
        greet(r + 1, False)

    turned = dot_tn(img_ref[...], perm_ref[...]).astype(BF)
    for hb in range(2):
        mine[hb] = turned[:, hb * 128 : (hb + 1) * 128]
        xbuf[d, 1 + hb, SIDE : SIDE + wdev, :] = turned[:, hb * 128 : (hb + 1) * 128]
    mkb[1 : 1 + own, :, 128 : 128 + wdev] = mk_ref[...]

    src_side = pl.multiple_of(cp * (wdev - SIDE), SIDE)
    dst_side = pl.multiple_of(c * (wdev + SIDE), SIDE)
    msrc_side = pl.multiple_of(128 + cp * (wdev - 128), 128)
    mdst_side = pl.multiple_of(c * (wdev + 128), 128)

    def image_copy(kind, src_d, dst_d, rr, sd):
        side = kind % 2
        where = kind // 2
        if where == 0:
            blocks, dst_blocks = pl.ds(0, 2), pl.ds(1, 2)
        elif where == 1:
            blocks, dst_blocks = pl.ds(0, 1), pl.ds(3, 1)
        else:
            blocks, dst_blocks = pl.ds(1, 1), pl.ds(0, 1)
        if side:
            a, b = pl.ds(src_side, SIDE), pl.ds(dst_side, SIDE)
        else:
            a, b = pl.ds(0, wdev), pl.ds(SIDE, wdev)
        return pltpu.make_async_remote_copy(
            src_ref=mine.at[blocks, a, :],
            dst_ref=xbuf.at[src_d, dst_blocks, b, :],
            send_sem=send_sem.at[kind * D + sd],
            recv_sem=recv_sem.at[kind * D + src_d],
            device_id={"rows": rr, "dates": dst_d, "cols": cp if side else c},
            device_id_type=pl.DeviceIdType.MESH,
        )

    def mask_copy(kind, to):
        side = kind % 2
        where = kind // 2
        if where == 0:
            a, b = pl.ds(1, own), pl.ds(1, own)
        elif where == 1:
            a, b = pl.ds(1, 1), pl.ds(own + 1, 1)
        else:
            a, b = pl.ds(own, 1), pl.ds(0, 1)
        if side:
            x, y = pl.ds(msrc_side, 128), pl.ds(mdst_side, 128)
        else:
            x, y = pl.ds(128, wdev), pl.ds(128, wdev)
        return pltpu.make_async_remote_copy(
            src_ref=mkb.at[a, :, x],
            dst_ref=mkb.at[b, :, y],
            send_sem=mask_send.at[kind],
            recv_sem=mask_recv.at[kind],
            device_id={"rows": to // D, "dates": lax.rem(to, D), "cols": cp if side else c},
            device_id_type=pl.DeviceIdType.MESH,
        )

    def needs_next(q):
        return own * q + own + 4 > strip

    def needs_prev(q):
        return own * q < 4

    greeted = 2 * D - 1 + 2 * D * ((r > 0).astype(jnp.int32) + (r < R - 1).astype(jnp.int32))
    pl.semaphore_wait(barrier, greeted)

    def sends(act):
        @pl.when(r > 0)
        def _():
            for k in range(D):
                to = lax.rem(d + k, D)

                @pl.when(needs_next(to))
                def _():
                    act(image_copy(2, d, to, r - 1, k))
                    act(image_copy(3, d, to, r - 1, k))

        @pl.when(r < R - 1)
        def _():
            for k in range(D):
                to = lax.rem(d + k, D)

                @pl.when(needs_prev(to))
                def _():
                    act(image_copy(4, d, to, r + 1, k))
                    act(image_copy(5, d, to, r + 1, k))

        for k in range(D):
            to = lax.rem(d + k, D)
            act(image_copy(1, d, to, r, k))
            if k > 0:
                act(image_copy(0, d, to, r, k))
        act(mask_copy(1, f))

        @pl.when(f > 0)
        def _():
            act(mask_copy(2, f - 1))
            act(mask_copy(3, f - 1))

        @pl.when(f < R * D - 1)
        def _():
            act(mask_copy(4, f + 1))
            act(mask_copy(5, f + 1))

    sends(lambda copy: copy.start())

    def arrived(k):
        source = lax.rem(d + k, D)
        image_copy(1, source, d, r, k).wait_recv()
        if k > 0:
            image_copy(0, source, d, r, k).wait_recv()

        @pl.when((r < R - 1) & needs_next(d))
        def _():
            image_copy(2, source, d, r, k).wait_recv()
            image_copy(3, source, d, r, k).wait_recv()

        @pl.when((r > 0) & needs_prev(d))
        def _():
            image_copy(4, source, d, r, k).wait_recv()
            image_copy(5, source, d, r, k).wait_recv()

    k1[...] = jnp.zeros_like(k1)
    for off in range(4):
        for dy in range(3):
            for dx in range(3):
                for o in range(2):
                    row = 2 * off + o + dy
                    at = (row // 8) * 384 + dx * 128 + (row % 8) * 16
                    k1[off, at : at + 16, o * 128 : (o + 1) * 128] = w1_ref[dy, dx]
    for w_ref, k_ref in ((w2_ref, k2), (w3_ref, k3), (wdec_ref, kd)):
        k_ref[...] = jnp.zeros_like(k_ref)
        for dy in range(3):
            for dx in range(3):
                for o in range(2):
                    at = (o + dy) * 384 + dx * 128
                    k_ref[at : at + 128, o * 128 : (o + 1) * 128] = w_ref[dy, dx]

    full = lax.dot_general(
        wkey_ref[...].astype(F32),
        q_ref[...],
        (((1,), (0,)), ((), ())),
        precision=lax.Precision.HIGHEST,
        preferred_element_type=F32,
    )
    high = full.astype(BF).astype(F32)
    lane = lax.broadcasted_iota(jnp.int32, full.shape, 1)
    both = jnp.where(lane < L, high, full - high)
    for t in range(T):
        mine_t = (lane % L) // heads == t
        ws[t * model : (t + 1) * model, :] = jnp.where(mine_t, both, 0.0).astype(BF)

    kk = lax.broadcasted_iota(jnp.int32, (512, 256), 0)
    nn = lax.broadcasted_iota(jnp.int32, (512, 256), 1)
    same = ((kk // 128) * 4 + (kk % 64) // 16 == d * own + nn // 16) & (kk % 16 == nn % 16)
    for p in range(dl):
        sel[p] = jnp.where(same & ((kk % 128) // 64 == p), 1.0, 0.0).astype(BF)

    px = lax.broadcasted_iota(jnp.int32, (M, 128), 0)
    at_col = px + (c * wdev - SIDE)
    inside = (at_col >= 0) & (at_col < 2 * wdev)
    col_mask = jnp.where(inside, 1.0, 0.0).astype(F32)
    first_row = r * strip + d * own

    def row_mask(rel):
        at = first_row + rel
        ok = ((at >= 0) & (at < height)).astype(F32)
        return ok

    def spread(y, into, base, rel):
        y = y * (col_mask * row_mask(rel))
        into[:, pl.ds(base, 128)] = pltpu.roll(y, 1, 0).astype(BF)
        into[:, pl.ds(base + 128, 128)] = y.astype(BF)
        into[:, pl.ds(base + 256, 128)] = pltpu.roll(y, M - 1, 0).astype(BF)

    def one_date(i, carry):
        t = lax.rem(d * dl + i, T)
        source = t // dl
        par = lax.rem(t, dl)
        window = dot(xbuf[source, 0], sel[par, 0:128, :])
        for b in range(1, 4):
            window = window + dot(xbuf[source, b], sel[par, b * 128 : (b + 1) * 128, :])
        for h in range(2):
            part = window[:, h * 128 : (h + 1) * 128]
            xw[:, h * 384 : h * 384 + 128] = pltpu.roll(part, 1, 0).astype(BF)
            xw[:, h * 384 + 128 : h * 384 + 256] = part.astype(BF)
            xw[:, h * 384 + 256 : h * 384 + 384] = pltpu.roll(part, M - 1, 0).astype(BF)
        for j in range((own + 6) // 2):
            at = (j // 4) * 384
            if j % 4 == 3:
                y = dot(xw[...], k1[3])
            else:
                y = dot(xw[:, at : at + 384], k1[j % 4, 0:384, :])
            for o in range(2):
                v = jnp.maximum(y[:, o * 128 : (o + 1) * 128] + b1_ref[...], 0.0)
                spread(v, s1, (2 * j + o) * 384, 2 * j + o - 3)
        for j in range((own + 4) // 2):
            y = dot(s1[:, j * 768 : j * 768 + 1536], k2[...])
            for o in range(2):
                v = jnp.maximum(y[:, o * 128 : (o + 1) * 128] + b2_ref[...], 0.0)
                spread(v, s2, (2 * j + o) * 384, 2 * j + o - 2)
        for j in range((own + 2) // 2):
            y = dot(s2[:, j * 768 : j * 768 + 1536], k3[...])
            for o in range(2):
                v = jnp.maximum(y[:, o * 128 : (o + 1) * 128] + b3_ref[...], 0.0)
                enc[t, :, (2 * j + o) * 128 : (2 * j + o + 1) * 128] = v.astype(BF)
        return carry

    for k in range(D):
        arrived(k)
        lax.fori_loop(k * dl, (k + 1) * dl, one_date, 0)

    mask_copy(1, f).wait_recv()

    @pl.when(f < R * D - 1)
    def _():
        mask_copy(2, f).wait_recv()
        mask_copy(3, f).wait_recv()

    @pl.when(f > 0)
    def _():
        mask_copy(4, f).wait_recv()
        mask_copy(5, f).wait_recv()

    def one_row(i, carry):
        at = pl.multiple_of(i * 128, 128)
        for t in range(T):
            v = dot(enc[t, :, pl.ds(at, 128)], win_ref[...]) + pos_ref[t : t + 1, :]
            pa[:, t * model : (t + 1) * model] = v.astype(BF)
        z = dot(pa[...], ws[...])
        raw = z + pltpu.roll(z, L, 1)
        extra = dot_tn(mkb[i], bsel_ref[...])[128 - SIDE : 128 + wdev + SIDE]
        w = jnp.exp(8.0 * jnp.tanh(raw * 0.125) + extra)
        total = w
        step = heads
        while step < L:
            total = total + pltpu.roll(total, step, 1)
            step *= 2
        att = (w / total).astype(BF)
        pooled = None
        for t in range(T):
            cols = slice(t * model, (t + 1) * model)
            term = dot(att, ex_ref[:, cols]) * pa[:, cols].astype(F32)
            pooled = term if pooled is None else pooled + term
        v = jnp.maximum(dot(pooled.astype(BF), wmlp_ref[...]) + bmlp_ref[...], 0.0)
        spread(v, s3, pl.multiple_of(i * 384, 128), i - 1)
        return carry

    lax.fori_loop(0, own + 2, one_row, 0)

    for j in range(own // 2):
        y = dot(s3[:, j * 768 : j * 768 + 1536], kd[...])
        for o in range(2):
            v = jnp.maximum(y[SIDE : SIDE + wdev, o * 128 : (o + 1) * 128] + bdec_ref[...], 0.0)
            res = dot_nt(wout_ref[...], v.astype(BF)) + bout_ref[...]
            out_ref[:, 2 * j + o, :] = res[0:bands]

    sends(lambda copy: copy.wait_send())


def on_device(
    axes,
    images,
    cloud_mask,
    counts,
    day_of_year,
    w_first,
    b_first,
    w_second,
    b_second,
    w_third,
    b_third,
    w_in,
    w_key,
    master_query,
    w_mlp,
    b_mlp,
    w_dec,
    b_dec,
    w_out,
    b_out,
):
    R, D = axes
    dl, bands, strip, wdev = images.shape
    own = counts.shape[0]
    T = cloud_mask.shape[0]
    heads, key_size = master_query.shape
    model = w_in.shape[1]
    L = T * heads
    M = wdev + 2 * SIDE
    chan = w_in.shape[0]
    cfg = (R, D, dl, own, strip, wdev, heads, model, bands)

    invalid = jnp.arange(T)[:, None, None] >= counts[None]
    mk = jnp.concatenate([cloud_mask.astype(BF), invalid.astype(BF)], axis=0)
    mk = jnp.pad(mk, ((0, 16 - 2 * T), (0, 0), (0, 0))).transpose(1, 0, 2)

    perm = np.zeros((dl * bands * strip, 256), np.float32)
    for p in range(dl):
        for ch in range(bands):
            for row in range(strip):
                lane = (row // 4) * 128 + p * 64 + (row % 4) * 16 + ch
                perm[(p * bands + ch) * strip + row, lane] = 1.0
    n = np.arange(2 * L)
    head_of = n % heads
    date_of = (n % L) // heads
    ex = np.zeros((2 * L, T * model), np.float32)
    for t in range(T):
        for m in range(model):
            ex[t * heads + m // (model // heads), t * model + m] = 1.0
    bsel = np.zeros((16, 2 * L), np.float32)
    for t in range(T):
        bsel[t, date_of == t] = -4.0
        bsel[T + t, date_of == t] = -1e30
    pick = (np.arange(heads * key_size)[:, None] // key_size == head_of[None, :]).astype(np.float32)
    q = master_query.reshape(heads * key_size, 1) * (pick / math.sqrt(key_size))

    args = (
        images.reshape(dl * bands * strip, wdev),
        mk,
        jnp.asarray(perm, BF),
        positions(day_of_year, model),
        jnp.pad(w_first, ((0, 0), (0, 0), (0, 16 - bands), (0, 0))),
        b_first[None],
        w_second,
        b_second[None],
        w_third,
        b_third[None],
        w_in,
        w_key,
        q,
        jnp.asarray(ex, BF),
        jnp.asarray(bsel, BF),
        w_mlp,
        b_mlp[None],
        w_dec,
        b_dec[None],
        jnp.pad(w_out, ((0, 16 - bands), (0, 0))),
        jnp.pad(b_out, (0, 16 - bands))[:, None],
    )
    return pl.pallas_call(
        functools.partial(kernel, cfg),
        out_shape=jax.ShapeDtypeStruct((bands, own, wdev), F32),
        in_specs=[pl.BlockSpec(memory_space=pltpu.VMEM)] * len(args),
        out_specs=pl.BlockSpec(memory_space=pltpu.VMEM),
        scratch_shapes=[
            pltpu.VMEM((2, wdev, 128), BF),
            pltpu.VMEM((D, 4, M, 128), BF),
            pltpu.VMEM((own + 2, 16, wdev + 256), BF),
            pltpu.VMEM((M, 768), BF),
            pltpu.VMEM((M, (own + 6) * 384), BF),
            pltpu.VMEM((M, (own + 4) * 384), BF),
            pltpu.VMEM((M, (own + 2) * 384), BF),
            pltpu.VMEM((T, M, (own + 2) * 128), BF),
            pltpu.VMEM((M, T * model), BF),
            pltpu.VMEM((4, 768, 256), BF),
            pltpu.VMEM((12 * chan, 2 * chan), BF),
            pltpu.VMEM((12 * chan, 2 * chan), BF),
            pltpu.VMEM((12 * chan, 2 * chan), BF),
            pltpu.VMEM((T * model, 2 * L), BF),
            pltpu.VMEM((dl, 512, 256), BF),
            pltpu.SemaphoreType.DMA((6 * D,)),
            pltpu.SemaphoreType.DMA((6 * D,)),
            pltpu.SemaphoreType.DMA((6,)),
            pltpu.SemaphoreType.DMA((6,)),
        ],
        compiler_params=pltpu.CompilerParams(
            collective_id=0, has_side_effects=True, vmem_limit_bytes=56 * 1024 * 1024
        ),
    )(*args)


def solution(mesh):
    placed = (
        P("dates", None, ("groups", "rows"), "cols"),
        P(None, ("groups", "rows", "dates"), "cols"),
        P(("groups", "rows", "dates"), "cols"),
        P("groups"),
    ) + (P(),) * 15
    return jax.shard_map(
        functools.partial(on_device, (mesh.shape["rows"], mesh.shape["dates"])),
        mesh=mesh,
        in_specs=placed,
        out_specs=P(None, ("groups", "rows", "dates"), "cols"),
        check_vma=False,
    )
```

profile of v0, /device:TPU:15, one launch (start us, length us, event | category | flops | bytes accessed | tf_op | source)
XLA Modules:
  0.0 53.7 jit_solution(16311274612826622134)
XLA Ops:
  0.0 0.7 %convert_element_type.26 = f32[4]{0:T(128)S(1)} convert(s32[4]{0:T(128)} %param.26) | non-fusion elementwise | flops 4 | bytes 32 | tf_op jit(solution)/shard_map/convert_element_type | solution.py:20
  0.7 0.1 multiply_sine_fusion
  0.8 0.2 copy.34
  1.0 0.0 copy-start.2
  1.0 0.7 %copy.36.pos_ref = f32[4,256]{1,0:T(4,128)} copy(f32[4,256]{0,1:T(8,128)S(1)} %bitcast.11) | data formatting | bytes 8192 | tf_op jit(solution)/shard_map/reshape | solution.py:21
  1.6 0.1 copy-done.2
  1.7 0.0 copy-start.4
  1.7 0.7 %copy-done.4 = s32[4,512]{1,0:T(4,128)S(1)} copy-done((s32[4,512]{1,0:T(4,128)S(1)}, s32[4,512]{1,0:T(4,128)}, u32[]{:S(2)}) %copy-start.4) | copy-done | bytes 8216
  2.4 0.0 copy-start.1
  2.4 0.7 %fusion.3.mk_ref = bf16[4,16,512]{2,1,0:T(8,128)(2,1)} fusion(bf16[4,4,512]{2,0,1:T(4,128)(2,1)S(1)} %fusion.4, bf16[4,4,512]{2,0,1:T(4,128)(2,1)S(1)} %copy_convert_fusion), kind=kLoop, calls=%fused_computation.4 | loop fusion | flops 229376 | bytes 98304 | tf_op jit(solution)/shard_map/transpose | solution.py:419
  3.1 0.1 copy-done.1
  3.2 0.0 copy-start.6
  3.2 0.0 copy-start.3
  3.2 0.7 %copy.37.wkey_ref = bf16[256,64]{1,0:T(8,128)(2,1)} copy(bf16[256,64]{0,1:T(8,128)(2,1)S(1)} %copy-done.1) | data formatting | bytes 65536 | tf_op args[11]
  3.9 0.0 copy-done.6
  3.9 0.1 copy.35
  4.0 0.0 copy-start
  4.0 0.1 mul.40
  4.1 0.0 copy-done.3
  4.1 0.7 %broadcast_multiply_fusion.q_ref = f32[64,128]{1,0:T(8,128)} fusion(f32[64,128]{1,0:T(8,128)S(1)} %copy-done.3, f32[64]{0:T(128)S(1)} %mul.40), kind=kLoop, calls=%fused_computation.8 | loop fusion | flops 8192 | bytes 65792 | tf_op jit(solution)/shard_map/mul | solution.py:439
  4.8 0.0 copy-done
  4.8 0.0 copy-start.7
  4.8 0.6 %pad.17.w1_ref = bf16[3,3,16,128]{3,2,1,0:T(8,128)(2,1)} pad(bf16[3,3,13,128]{3,2,1,0:T(8,128)(2,1)S(1)} %copy-done, bf16[]{:T(256)} %constant.16.clone.1), padding=0_0x0_0x0_3x0_0 | pad | bytes 66818 | tf_op jit(solution)/shard_map/jit(_pad)/pad | solution.py:446
  5.4 0.0 copy-done.7
  5.4 0.0 copy-start.5
  5.4 0.7 %copy.38.bout_ref = f32[16,1]{1,0:T(8,128)} copy(f32[16,1]{0,1:T(1,128)S(1)} %pad_bitcast_fusion) | data formatting | bytes 128 | tf_op jit(solution)/shard_map/broadcast_in_dim | solution.py:462
  6.1 0.0 copy-done.5
  6.1 0.6 %pad.18.wout_ref = bf16[16,128]{1,0:T(8,128)(2,1)} pad(bf16[13,128]{1,0:T(8,128)(2,1)S(1)} %copy-done.5, bf16[]{:T(256)} %constant.16.clone.1), padding=0_3x0_0 | pad | bytes 7426 | tf_op jit(solution)/shard_map/jit(_pad)/pad | solution.py:461
  6.7 45.4 %shard_map.217 = f32[13,4,512]{2,1,0:T(4,128)} custom-call(bf16[208,512]{1,0:T(8,128)(2,1)} %bitcast.12, bf16[4,16,512]{2,1,0:T(8,128)(2,1)} %fusion.3.mk_ref, bf16[208,256]{1,0:T(8,128)(2,1)} %constant.21.clone.perm_ref, f32[4,256]{1,0:T(4,128)} %copy.36.pos_ref, bf16[3,3,16,128]{3,2,1,0:T(8,128)(2,1)} %pad.17.w1_ref, f32[1,128]{1,0:T(1,128)} %bitcast.13, ...), custom_call_target="tpu_custom_call" | custom-call | tf_op jit(solution)/shard_map/pallas_call | solution.py:464
  52.2 1.5 %copy.41 = f32[13,4,512]{2,1,0:T(4,128)} copy(f32[13,4,512]{2,1,0:T(4,128)} %shard_map.217) | data formatting | bytes 212992
  (5 shorter events, 0.0 us)
Async XLA Ops:
  1.0 0.8 %copy-start.2 = (s32[4,4,512]{2,1,0:T(4,128)S(1)}, s32[4,4,512]{2,1,0:T(4,128)}, u32[]{:S(2)}) copy-start(s32[4,4,512]{2,1,0:T(4,128)} %param.24) | copy-start | bytes 98308
  1.7 0.7 %copy-start.4 = (s32[4,512]{1,0:T(4,128)S(1)}, s32[4,512]{1,0:T(4,128)}, u32[]{:S(2)}) copy-start(s32[4,512]{1,0:T(4,128)} %param.25) | copy-start | bytes 24580
  2.4 0.8 %copy-start.1 = (bf16[256,64]{0,1:T(8,128)(2,1)S(1)}, bf16[256,64]{0,1:T(8,128)(2,1)}, u32[]{:S(2)}) copy-start(bf16[256,64]{0,1:T(8,128)(2,1)} %param.34) | copy-start | bytes 98308
  3.2 0.7 %copy-start.6 = (f32[16,4]{0,1:T(4,128)S(1)}, f32[16,4]{0,1:T(4,128)}, u32[]{:S(2)}) copy-start(f32[16,4]{0,1:T(4,128)} %param.35) | copy-start | bytes 772
  3.2 0.9 %copy-start.3 = (f32[64,128]{1,0:T(8,128)S(1)}, f32[64,128]{1,0:T(8,128)}, u32[]{:S(2)}) copy-start(f32[64,128]{1,0:T(8,128)} %constant.20.clone) | copy-start | bytes 98308
  4.0 0.8 %copy-start = (bf16[3,3,13,128]{3,2,1,0:T(8,128)(2,1)S(1)}, bf16[3,3,13,128]{3,2,1,0:T(8,128)(2,1)}, u32[]{:S(2)}) copy-start(bf16[3,3,13,128]{3,2,1,0:T(8,128)(2,1)} %param.27) | copy-start | bytes 89860
  4.8 0.7 %copy-start.7 = (f32[13]{0:T(128)S(1)}, f32[13]{0:T(128)}, u32[]{:S(2)}) copy-start(f32[13]{0:T(128)} %param.41) | copy-start | bytes 160
  5.4 0.7 %copy-start.5 = (bf16[13,128]{1,0:T(8,128)(2,1)S(1)}, bf16[13,128]{1,0:T(8,128)(2,1)}, u32[]{:S(2)}) copy-start(bf16[13,128]{1,0:T(8,128)(2,1)} %param.40) | copy-start | bytes 9988
where the time goes:
time: 54.2 us; the launch traced here: 53.7 us
  Pallas kernels  45.4 us (84%)
  local copies, waits for them, and re-layouts  6.08 us (11%)
  other arithmetic  2.14 us (4%)
    pallas_call x1, Pallas kernels, on_device(): pl.pallas_call(functools.partial(kernel, cfg), out_shape=jax.ShapeDtypeSt...  45.4 us
    unnamed x19, local copies, waits for them, and re-layouts  3.27 us

commit v1 on v0

--- a/solution.py
+++ b/solution.py
@@ -14,15 +14,6 @@
 F32 = jnp.float32
 
 
-def positions(day_of_year, width_model):
-    channel = jnp.arange(width_model // 2).astype(F32)
-    frequency = jnp.power(F32(1000.0), -2.0 * channel / width_model)
-    angle_table = day_of_year.astype(F32)[:, None] * frequency[None, :]
-    return jnp.stack([jnp.sin(angle_table), jnp.cos(angle_table)], axis=-1).reshape(
-        day_of_year.shape[0], width_model
-    )
-
-
 def dot(a, b):
     return jnp.dot(a, b, preferred_element_type=F32)
 
@@ -38,9 +29,11 @@
 def kernel(
     cfg,
     img_ref,
-    mk_ref,
+    cloud_ref,
+    counts_ref,
+    day_ref,
+    freq_ref,
     perm_ref,
-    pos_ref,
     w1_ref,
     b1_ref,
     w2_ref,
@@ -49,7 +42,7 @@
     b3_ref,
     win_ref,
     wkey_ref,
-    q_ref,
+    query_ref,
     ex_ref,
     bsel_ref,
     wmlp_ref,
@@ -57,7 +50,6 @@
     wdec_ref,
     bdec_ref,
     wout_ref,
-    bout_ref,
     out_ref,
     mine,
     xbuf,
@@ -74,6 +66,8 @@
     kd,
     ws,
     sel,
+    pos_ref,
+    posr_ref,
     send_sem,
     recv_sem,
     mask_send,
@@ -127,8 +121,6 @@
     for hb in range(2):
         mine[hb] = turned[:, hb * 128 : (hb + 1) * 128]
         xbuf[d, 1 + hb, SIDE : SIDE + wdev, :] = turned[:, hb * 128 : (hb + 1) * 128]
-    mkb[1 : 1 + own, :, 128 : 128 + wdev] = mk_ref[...]
-
     src_side = pl.multiple_of(cp * (wdev - SIDE), SIDE)
     dst_side = pl.multiple_of(c * (wdev + SIDE), SIDE)
     msrc_side = pl.multiple_of(128 + cp * (wdev - 128), 128)
@@ -213,6 +205,8 @@
             act(image_copy(1, d, to, r, k))
             if k > 0:
                 act(image_copy(0, d, to, r, k))
+
+    def mask_sends(act):
         act(mask_copy(1, f))
 
         @pl.when(f > 0)
@@ -226,6 +220,17 @@
             act(mask_copy(5, f + 1))
 
     sends(lambda copy: copy.start())
+    date_no = lax.broadcasted_iota(jnp.int32, (T, wdev), 0)
+    for row in range(own):
+        rows = [
+            cloud_ref[:, row, :].astype(F32),
+            jnp.where(date_no >= counts_ref[row : row + 1, :], 1.0, 0.0).astype(F32),
+        ]
+        if 2 * T < 16:
+            rows.append(jnp.zeros((16 - 2 * T, wdev), F32))
+        mkb[1 + row, :, 128 : 128 + wdev] = jnp.concatenate(rows, axis=0).astype(BF)
+
+    mask_sends(lambda copy: copy.start())
 
     def arrived(k):
         source = lax.rem(d + k, D)
@@ -250,7 +255,7 @@
                 for o in range(2):
                     row = 2 * off + o + dy
                     at = (row // 8) * 384 + dx * 128 + (row % 8) * 16
-                    k1[off, at : at + 16, o * 128 : (o + 1) * 128] = w1_ref[dy, dx]
+                    k1[off, at : at + bands, o * 128 : (o + 1) * 128] = w1_ref[dy, dx]
     for w_ref, k_ref in ((w2_ref, k2), (w3_ref, k3), (wdec_ref, kd)):
         k_ref[...] = jnp.zeros_like(k_ref)
         for dy in range(3):
@@ -259,19 +264,39 @@
                     at = (o + dy) * 384 + dx * 128
                     k_ref[at : at + 128, o * 128 : (o + 1) * 128] = w_ref[dy, dx]
 
-    full = lax.dot_general(
-        wkey_ref[...].astype(F32),
-        q_ref[...],
-        (((1,), (0,)), ((), ())),
-        precision=lax.Precision.HIGHEST,
-        preferred_element_type=F32,
-    )
-    high = full.astype(BF).astype(F32)
-    lane = lax.broadcasted_iota(jnp.int32, full.shape, 1)
-    both = jnp.where(lane < L, high, full - high)
+    even = lax.broadcasted_iota(jnp.int32, (1, model), 1) % 2 == 0
     for t in range(T):
-        mine_t = (lane % L) // heads == t
-        ws[t * model : (t + 1) * model, :] = jnp.where(mine_t, both, 0.0).astype(BF)
+        angle = day_ref[t].astype(F32) * freq_ref[...]
+        pos_ref[t : t + 1, :] = jnp.where(even, jnp.sin(angle), jnp.cos(angle))
+    hk = wkey_ref.shape[0]
+    key_size = hk // heads
+
+    def exact(a, b, dims):
+        return lax.dot_general(
+            a, b, (dims, ((), ())), precision=lax.Precision.HIGHEST, preferred_element_type=F32
+        )
+
+    owner = lax.broadcasted_iota(jnp.int32, (hk, heads), 0) // key_size
+    owner = jnp.where(owner == lax.broadcasted_iota(jnp.int32, (hk, heads), 1), 1.0, 0.0)
+    each = exact(owner.astype(F32), query_ref[...], ((1,), (1,)))
+    place = lax.broadcasted_iota(jnp.int32, (hk, key_size), 0) % key_size
+    place = place == lax.broadcasted_iota(jnp.int32, (hk, key_size), 1)
+    column = jnp.sum(jnp.where(place, each, 0.0), axis=1, keepdims=True)
+    pick = lax.broadcasted_iota(jnp.int32, (hk, 2 * L), 0) // key_size
+    pick = pick == lax.broadcasted_iota(jnp.int32, (hk, 2 * L), 1) % heads
+    q = jnp.where(pick, column * (1.0 / math.sqrt(key_size)), 0.0)
+    full = exact(wkey_ref[...].astype(F32), q, ((0,), (0,)))
+    folded = exact(win_ref[...].astype(F32), full, ((1,), (0,)))
+    high = folded.astype(BF).astype(F32)
+    lane = lax.broadcasted_iota(jnp.int32, folded.shape, 1)
+    both = jnp.where(lane < L, high, folded - high)
+    chan = folded.shape[0]
+    for t in range(T):
+        ws[t * chan : (t + 1) * chan, :] = jnp.where((lane % L) // heads == t, both, 0.0).astype(BF)
+    shift = exact(pos_ref[...], full, ((1,), (0,)))
+    lane_t = (lax.broadcasted_iota(jnp.int32, shift.shape, 1) % L) // heads
+    shift = jnp.where(lane_t == lax.broadcasted_iota(jnp.int32, shift.shape, 0), shift, 0.0)
+    posr_ref[...] = jnp.sum(shift, axis=0, keepdims=True)
 
     kk = lax.broadcasted_iota(jnp.int32, (512, 256), 0)
     nn = lax.broadcasted_iota(jnp.int32, (512, 256), 1)
@@ -326,7 +351,7 @@
             y = dot(s2[:, j * 768 : j * 768 + 1536], k3[...])
             for o in range(2):
                 v = jnp.maximum(y[:, o * 128 : (o + 1) * 128] + b3_ref[...], 0.0)
-                enc[t, :, (2 * j + o) * 128 : (2 * j + o + 1) * 128] = v.astype(BF)
+                enc[2 * j + o, :, pl.ds(pl.multiple_of(t * 128, 128), 128)] = v.astype(BF)
         return carry
 
     for k in range(D):
@@ -345,13 +370,12 @@
         mask_copy(4, f).wait_recv()
         mask_copy(5, f).wait_recv()
 
-    def one_row(i, carry):
-        at = pl.multiple_of(i * 128, 128)
+    for i in range(own + 2):
+        z = dot(enc[i], ws[...])
         for t in range(T):
-            v = dot(enc[t, :, pl.ds(at, 128)], win_ref[...]) + pos_ref[t : t + 1, :]
-            pa[:, t * model : (t + 1) * model] = v.astype(BF)
-        z = dot(pa[...], ws[...])
-        raw = z + pltpu.roll(z, L, 1)
+            v = dot(enc[i, :, t * 128 : (t + 1) * 128], win_ref[...]) + pos_ref[t : t + 1, :]
+            pa[i % 2, :, t * model : (t + 1) * model] = v.astype(BF)
+        raw = z + pltpu.roll(z, L, 1) + posr_ref[...]
         extra = dot_tn(mkb[i], bsel_ref[...])[128 - SIDE : 128 + wdev + SIDE]
         w = jnp.exp(8.0 * jnp.tanh(raw * 0.125) + extra)
         total = w
@@ -363,22 +387,19 @@
         pooled = None
         for t in range(T):
             cols = slice(t * model, (t + 1) * model)
-            term = dot(att, ex_ref[:, cols]) * pa[:, cols].astype(F32)
+            term = dot(att, ex_ref[:, cols]) * pa[i % 2, :, cols].astype(F32)
             pooled = term if pooled is None else pooled + term
         v = jnp.maximum(dot(pooled.astype(BF), wmlp_ref[...]) + bmlp_ref[...], 0.0)
-        spread(v, s3, pl.multiple_of(i * 384, 128), i - 1)
-        return carry
-
-    lax.fori_loop(0, own + 2, one_row, 0)
+        spread(v, s3, i * 384, i - 1)
 
     for j in range(own // 2):
         y = dot(s3[:, j * 768 : j * 768 + 1536], kd[...])
         for o in range(2):
             v = jnp.maximum(y[SIDE : SIDE + wdev, o * 128 : (o + 1) * 128] + bdec_ref[...], 0.0)
-            res = dot_nt(wout_ref[...], v.astype(BF)) + bout_ref[...]
-            out_ref[:, 2 * j + o, :] = res[0:bands]
+            out_ref[:, 2 * j + o, :] = dot_nt(wout_ref[...], v.astype(BF))
 
     sends(lambda copy: copy.wait_send())
+    mask_sends(lambda copy: copy.wait_send())
 
 
 def on_device(
@@ -414,10 +435,6 @@
     chan = w_in.shape[0]
     cfg = (R, D, dl, own, strip, wdev, heads, model, bands)
 
-    invalid = jnp.arange(T)[:, None, None] >= counts[None]
-    mk = jnp.concatenate([cloud_mask.astype(BF), invalid.astype(BF)], axis=0)
-    mk = jnp.pad(mk, ((0, 16 - 2 * T), (0, 0), (0, 0))).transpose(1, 0, 2)
-
     perm = np.zeros((dl * bands * strip, 256), np.float32)
     for p in range(dl):
         for ch in range(bands):
@@ -425,7 +442,6 @@
                 lane = (row // 4) * 128 + p * 64 + (row % 4) * 16 + ch
                 perm[(p * bands + ch) * strip + row, lane] = 1.0
     n = np.arange(2 * L)
-    head_of = n % heads
     date_of = (n % L) // heads
     ex = np.zeros((2 * L, T * model), np.float32)
     for t in range(T):
@@ -435,36 +451,38 @@
     for t in range(T):
         bsel[t, date_of == t] = -4.0
         bsel[T + t, date_of == t] = -1e30
-    pick = (np.arange(heads * key_size)[:, None] // key_size == head_of[None, :]).astype(np.float32)
-    q = master_query.reshape(heads * key_size, 1) * (pick / math.sqrt(key_size))
+    freq = np.power(1000.0, -2.0 * (np.arange(model) // 2) / model).astype(np.float32)[None]
 
     args = (
         images.reshape(dl * bands * strip, wdev),
-        mk,
+        cloud_mask,
+        counts,
+        day_of_year,
+        jnp.asarray(freq),
         jnp.asarray(perm, BF),
-        positions(day_of_year, model),
-        jnp.pad(w_first, ((0, 0), (0, 0), (0, 16 - bands), (0, 0))),
+        w_first,
         b_first[None],
         w_second,
         b_second[None],
         w_third,
         b_third[None],
         w_in,
-        w_key,
-        q,
+        w_key.T,
+        master_query.T,
         jnp.asarray(ex, BF),
         jnp.asarray(bsel, BF),
         w_mlp,
         b_mlp[None],
         w_dec,
         b_dec[None],
-        jnp.pad(w_out, ((0, 16 - bands), (0, 0))),
-        jnp.pad(b_out, (0, 16 - bands))[:, None],
+        w_out,
     )
-    return pl.pallas_call(
+    specs = [pl.BlockSpec(memory_space=pltpu.VMEM)] * len(args)
+    specs[3] = pl.BlockSpec(memory_space=pltpu.SMEM)
+    out = pl.pallas_call(
         functools.partial(kernel, cfg),
         out_shape=jax.ShapeDtypeStruct((bands, own, wdev), F32),
-        in_specs=[pl.BlockSpec(memory_space=pltpu.VMEM)] * len(args),
+        in_specs=specs,
         out_specs=pl.BlockSpec(memory_space=pltpu.VMEM),
         scratch_shapes=[
             pltpu.VMEM((2, wdev, 128), BF),
@@ -474,14 +492,16 @@
             pltpu.VMEM((M, (own + 6) * 384), BF),
             pltpu.VMEM((M, (own + 4) * 384), BF),
             pltpu.VMEM((M, (own + 2) * 384), BF),
-            pltpu.VMEM((T, M, (own + 2) * 128), BF),
-            pltpu.VMEM((M, T * model), BF),
+            pltpu.VMEM((own + 2, M, T * chan), BF),
+            pltpu.VMEM((2, M, T * model), BF),
             pltpu.VMEM((4, 768, 256), BF),
             pltpu.VMEM((12 * chan, 2 * chan), BF),
             pltpu.VMEM((12 * chan, 2 * chan), BF),
             pltpu.VMEM((12 * chan, 2 * chan), BF),
-            pltpu.VMEM((T * model, 2 * L), BF),
+            pltpu.VMEM((T * chan, 2 * L), BF),
             pltpu.VMEM((dl, 512, 256), BF),
+            pltpu.VMEM((T, model), F32),
+            pltpu.VMEM((1, 2 * L), F32),
             pltpu.SemaphoreType.DMA((6 * D,)),
             pltpu.SemaphoreType.DMA((6 * D,)),
             pltpu.SemaphoreType.DMA((6,)),
@@ -491,6 +511,7 @@
             collective_id=0, has_side_effects=True, vmem_limit_bytes=56 * 1024 * 1024
         ),
     )(*args)
+    return out + b_out[:, None, None]
 
 
 def solution(mesh):

time: 54.2 us -> 42.2 us (0.78)
  local copies, waits for them, and re-layouts: 6.08 us -> 0.01 us
  Pallas kernels: 45.4 us -> 40.4 us
    pallas_call x1, Pallas kernels: 45.4 us -> 40.4 us  [on_device(): pl.pallas_call(functools.partial(kernel, cfg), out_shape=jax.ShapeDtypeSt...]
    unnamed x19 -> x2, local copies, waits for them, and re-layouts: 3.27 us -> 0.01 us
    add x0 -> x1, other arithmetic: none -> 1.62 us  [on_device(): return out + b_out[:, None, None]]
    pad x2 -> x0, local copies, waits for them, and re-layouts: 1.22 us -> none  [the longest x1 0.62 us: on_device(): jnp.pad(w_first, ((0, 0), (0, 0), (0, 16 - bands), (0, 0)))]
    convert_element_type x3 -> x0, other arithmetic: 0.68 us -> none  [the longest x1 0.66 us: positions(): angle_table = day_of_year.astype(F32)[:, None] * frequency[None, :]]
    mul x1 -> x0, other arithmetic: 0.68 us -> none  [on_device(): q = master_query.reshape(heads * key_size, 1) * (pick / math.sqrt(key_size))]
    broadcast_in_dim x2 -> x0, local copies, waits for them, and re-layouts: 0.68 us -> none  [on_device(): jnp.pad(b_out, (0, 16 - bands))[:, None]]
    reshape x1 -> x0, local copies, waits for them, and re-layouts: 0.67 us -> none  [positions(): jnp.stack([jnp.sin(angle_table), jnp.cos(angle_table)], axis=-1)]
where the time goes in v1:
time: 42.2 us; the launch traced here: 42.1 us
  Pallas kernels  40.4 us (96%)
  other arithmetic  1.62 us (4%)
    pallas_call x1, Pallas kernels, on_device(): pl.pallas_call(functools.partial(kernel, cfg), out_shape=jax.ShapeDtypeSt...  40.4 us
    add x1, other arithmetic, on_device(): return out + b_out[:, None, None]  1.62 us

profile of v1, /device:TPU:15, one launch (start us, length us, event | category | flops | bytes accessed | tf_op | source)
XLA Modules:
  0.0 42.1 jit_solution(16517871817793655691)
XLA Ops:
  0.0 0.0 copy-start
  0.0 40.4 %shard_map.217 = f32[13,4,512]{2,1,0:T(4,128)} custom-call(bf16[208,512]{1,0:T(8,128)(2,1)} %bitcast.8, s32[4,4,512]{2,1,0:T(4,128)} %cloud_ref.1, s32[4,512]{1,0:T(4,128)} %counts_ref.1, s32[4]{0:T(128)} %day_ref.1, f32[1,256]{1,0:T(1,128)} %constant.8.clone.freq_ref, bf16[208,256]{1,0:T(8,128)(2,1)} %constant.9.clone.perm_ref, ...), custom_call_target="tpu_custom_call" | custom-call | tf_op jit(solution)/shard_map/pallas_call | solution.py:482
  40.4 0.0 copy-done
  40.4 1.6 %broadcast_add_fusion = f32[13,4,512]{2,1,0:T(4,128)} fusion(f32[13,4,512]{2,1,0:T(4,128)} %shard_map.217, f32[13]{0:T(128)S(1)} %copy-done), kind=kLoop, calls=%fused_computation | loop fusion | flops 26624 | bytes 213044 | tf_op jit(solution)/shard_map/add | solution.py:514
Async XLA Ops:
  0.0 40.4 %copy-start = (f32[13]{0:T(128)S(1)}, f32[13]{0:T(128)}, u32[]{:S(2)}) copy-start(f32[13]{0:T(128)} %param.41) | copy-start | bytes 160
